TPU v7x, 32 devices: a whole 2x2x4 slice. The times are simulated.
32 devices in a mesh: dp: 32 (over z, y, x, core).
Axes of the slice: x: 2, y: 2, z: 4, core: 2. Of those that a mesh axis runs over, the one named last changes fastest.
Arguments:
- tokens: bfloat16 [65536, 768], P('dp'), may hold values from -6 to 6
- norm_gain: bfloat16 [768], P('dp'), may hold values from 0.099609375 to 1.8984375
- norm_shift: bfloat16 [768], P('dp'), may hold values from -1.75 to 1.75
- query_weight: bfloat16 [768, 768], P('dp'), may hold values from -0.21875 to 0.21875
- query_bias: bfloat16 [768], P('dp'), may hold values from -1.75 to 1.75
- key_weight: bfloat16 [768, 768], P('dp'), may hold values from -0.21875 to 0.21875
- value_weight: bfloat16 [768, 768], P('dp'), may hold values from -0.21875 to 0.21875
- value_bias: bfloat16 [768], P('dp'), may hold values from -1.75 to 1.75
- output_weight: bfloat16 [768, 768], P('dp'), may hold values from -1.25 to 1.25
- output_bias: bfloat16 [768], P('dp'), may hold values from -1.75 to 1.75
- second_gain: bfloat16 [768], P('dp'), may hold values from 0.099609375 to 1.8984375
- second_shift: bfloat16 [768], P('dp'), may hold values from -1.75 to 1.75
- up_weight: bfloat16 [768, 3072], P('dp'), may hold values from -0.21875 to 0.21875
- up_bias: bfloat16 [3072], P('dp'), may hold values from -3 to 3
- down_weight: bfloat16 [3072, 768], P('dp'), may hold values from -0.109375 to 0.109375
- down_bias: bfloat16 [768], P('dp'), may hold values from -1.75 to 1.75
- cotangent: bfloat16 [65536, 768], P('dp'), may hold values from -12 to 12
Outputs:
- mixed: bfloat16 [65536, 768], P('dp')
- input_grad: float32 [65536, 768], P('dp')
- grad_norm_gain: float32 [768], P('dp')
- grad_norm_shift: float32 [768], P('dp')
- grad_query_weight: float32 [768, 768], P('dp')
- grad_query_bias: float32 [768], P('dp')
- grad_key_weight: float32 [768, 768], P('dp')
- grad_value_weight: float32 [768, 768], P('dp')
- grad_value_bias: float32 [768], P('dp')
- grad_output_weight: float32 [768, 768], P('dp')
- grad_output_bias: float32 [768], P('dp')
- grad_second_gain: float32 [768], P('dp')
- grad_second_shift: float32 [768], P('dp')
- grad_up_weight: float32 [768, 3072], P('dp')
- grad_up_bias: float32 [3072], P('dp')
- grad_down_weight: float32 [3072, 768], P('dp')
- grad_down_bias: float32 [768], P('dp')
All inputs are finite; a program needn't handle non-finite values.
Results may differ from a plain program's by a relative error of at most 0.011.
Values may be sent and summed in bfloat16 or wider, within the bound.
No kernel may reach another device: no remote copies, remote signals or barrier semaphores. Data moves between devices by JAX's collectives and lax.ppermute only.
A program may use at most 384 MiB of HBM per device.

v0:
```python
import jax
import jax.numpy as jnp
from jax import lax
from jax.sharding import PartitionSpec as P

HD = 64
SEQ = 1024


epsilon = 1e-05


def layer_norm(values, gain, shift):
    center = values - jnp.mean(values, axis=-1, keepdims=True)
    spread = jnp.mean(center * center, axis=-1, keepdims=True)
    return center * lax.rsqrt(spread + epsilon) * gain + shift


def smooth_act(values):
    return jax.nn.gelu(values, approximate=True)


def dense_mul(left, right):
    return jnp.dot(left, right, preferred_element_type=jnp.float32)


def outer_mul(left, right):
    return lax.dot_general(
        left, right, (((0,), (0,)), ((), ())), preferred_element_type=jnp.float32
    )


def back_mul(left, right):
    return lax.dot_general(
        left, right, (((1,), (1,)), ((), ())), preferred_element_type=jnp.float32
    )


def split_heads(values):
    return values.reshape(values.shape[0], values.shape[1] // HD, HD)


def causal_mask(row_start, block_rows, key_count):
    rows_idx = row_start + jnp.arange(block_rows)[:, None]
    cols_idx = jnp.arange(key_count)[None, :]
    return cols_idx <= rows_idx


def block_scores(query_heads, key_heads, row_start, row_end):
    scaling = HD ** (-0.5)
    scores = (
        jnp.einsum(
            "qhd,khd->hqk",
            query_heads[row_start:row_end],
            key_heads[:row_end],
            preferred_element_type=jnp.float32,
        )
        * scaling
    )
    allowed = causal_mask(row_start, row_end - row_start, row_end)
    return jnp.where(allowed[None], scores, -jnp.inf)


def attention_forward(queries, keys_low, values_low):
    seq_len = queries.shape[0]
    block_rows = min(512, seq_len)
    query_heads = split_heads(queries)
    key_heads = split_heads(keys_low)
    value_heads = split_heads(values_low)
    outputs = []
    totals = []
    for row_start in range(0, seq_len, block_rows):
        row_end = row_start + block_rows
        scores = block_scores(query_heads, key_heads, row_start, row_end)
        row_max = jnp.max(scores, axis=-1, keepdims=True)
        log_total = row_max + jnp.log(jnp.sum(jnp.exp(scores - row_max), axis=-1, keepdims=True))
        probs = jnp.exp(scores - log_total).astype(jnp.bfloat16)
        outputs.append(
            jnp.einsum(
                "hqk,khd->qhd", probs, value_heads[:row_end], preferred_element_type=jnp.float32
            )
        )
        totals.append(log_total)
    merged = jnp.concatenate(outputs, axis=0)
    return (merged.reshape(seq_len, queries.shape[1]), totals)


def attention_backward(queries, keys_low, values_low, totals, grad_attn):
    seq_len = queries.shape[0]
    block_rows = min(512, seq_len)
    scaling = HD ** (-0.5)
    query_heads = split_heads(queries)
    key_heads = split_heads(keys_low)
    value_heads = split_heads(values_low)
    grad_heads = split_heads(grad_attn)
    query_parts = []
    grad_keys = jnp.zeros(key_heads.shape, jnp.float32)
    grad_values = jnp.zeros(value_heads.shape, jnp.float32)
    for block_index, row_start in enumerate(range(0, seq_len, block_rows)):
        row_end = row_start + block_rows
        scores = block_scores(query_heads, key_heads, row_start, row_end)
        probs_full = jnp.exp(scores - totals[block_index])
        probs_low = probs_full.astype(jnp.bfloat16)
        grad_probs = jnp.einsum(
            "qhd,khd->hqk",
            grad_heads[row_start:row_end],
            value_heads[:row_end],
            preferred_element_type=jnp.float32,
        )
        inner = jnp.sum(grad_probs * probs_full, axis=-1, keepdims=True)
        grad_scores = (probs_full * (grad_probs - inner)).astype(jnp.bfloat16)
        query_parts.append(
            jnp.einsum(
                "hqk,khd->qhd", grad_scores, key_heads[:row_end], preferred_element_type=jnp.float32
            )
            * scaling
        )
        grad_keys = grad_keys.at[:row_end].add(
            jnp.einsum(
                "hqk,qhd->khd",
                grad_scores,
                query_heads[row_start:row_end],
                preferred_element_type=jnp.float32,
            )
            * scaling
        )
        grad_values = grad_values.at[:row_end].add(
            jnp.einsum(
                "hqk,qhd->khd",
                probs_low,
                grad_heads[row_start:row_end],
                preferred_element_type=jnp.float32,
            )
        )
    width = queries.shape[1]
    grad_queries = jnp.concatenate(query_parts, axis=0).reshape(seq_len, width)
    return (grad_queries, grad_keys.reshape(seq_len, width), grad_values.reshape(seq_len, width))


def forward_pass(inputs, weights):
    (
        norm_gain,
        norm_shift,
        query_weight,
        query_bias,
        key_weight,
        value_weight,
        value_bias,
        output_weight,
        output_bias,
        second_gain,
        second_shift,
        up_weight,
        up_bias,
        down_weight,
        down_bias,
    ) = weights
    start_vals = inputs.astype(jnp.float32)
    normed = layer_norm(
        start_vals, norm_gain.astype(jnp.float32), norm_shift.astype(jnp.float32)
    ).astype(jnp.bfloat16)
    queries = (dense_mul(normed, query_weight) + query_bias.astype(jnp.float32)).astype(
        jnp.bfloat16
    )
    keys_low = dense_mul(normed, key_weight).astype(jnp.bfloat16)
    values_low = (dense_mul(normed, value_weight) + value_bias.astype(jnp.float32)).astype(
        jnp.bfloat16
    )
    attended, totals = attention_forward(queries, keys_low, values_low)
    attn_low = attended.astype(jnp.bfloat16)
    residual = start_vals + dense_mul(attn_low, output_weight) + output_bias.astype(jnp.float32)
    second = layer_norm(
        residual, second_gain.astype(jnp.float32), second_shift.astype(jnp.float32)
    ).astype(jnp.bfloat16)
    hidden = dense_mul(second, up_weight) + up_bias.astype(jnp.float32)
    active = smooth_act(hidden).astype(jnp.bfloat16)
    result = residual + dense_mul(active, down_weight) + down_bias.astype(jnp.float32)
    stored = (
        start_vals,
        normed,
        queries,
        keys_low,
        values_low,
        totals,
        attn_low,
        residual,
        second,
        hidden,
        active,
    )
    return (stored, result.astype(jnp.bfloat16))


def backward_pass(stored, weights, cot_rows):
    (
        norm_gain,
        norm_shift,
        query_weight,
        query_bias,
        key_weight,
        value_weight,
        value_bias,
        output_weight,
        output_bias,
        second_gain,
        second_shift,
        up_weight,
        up_bias,
        down_weight,
        down_bias,
    ) = weights
    (
        start_vals,
        normed,
        queries,
        keys_low,
        values_low,
        totals,
        attn_low,
        residual,
        second,
        hidden,
        active,
    ) = stored
    grad_out = cot_rows.astype(jnp.float32)
    grad_down_bias = jnp.sum(grad_out, axis=0)
    grad_down_weight = outer_mul(active, cot_rows)
    grad_active = back_mul(cot_rows, down_weight)
    unused, gelu_pull = jax.vjp(smooth_act, hidden)
    grad_hidden = gelu_pull(grad_active)[0].astype(jnp.bfloat16)
    grad_up_bias = jnp.sum(grad_hidden.astype(jnp.float32), axis=0)
    grad_up_weight = outer_mul(second, grad_hidden)
    grad_second = back_mul(grad_hidden, up_weight)
    unused, second_pull = jax.vjp(
        layer_norm, residual, second_gain.astype(jnp.float32), second_shift.astype(jnp.float32)
    )
    grad_resid_norm, grad_second_gain, grad_second_shift = second_pull(grad_second)
    grad_residual = grad_out + grad_resid_norm
    grad_branch = grad_residual.astype(jnp.bfloat16)
    grad_output_bias = jnp.sum(grad_branch.astype(jnp.float32), axis=0)
    grad_output_weight = outer_mul(attn_low, grad_branch)
    grad_attn = back_mul(grad_branch, output_weight).astype(jnp.bfloat16)
    grad_queries, grad_keys, grad_values = attention_backward(
        queries, keys_low, values_low, totals, grad_attn
    )
    query_grad_low = grad_queries.astype(jnp.bfloat16)
    key_grad_low = grad_keys.astype(jnp.bfloat16)
    value_grad_low = grad_values.astype(jnp.bfloat16)
    grad_query_weight = outer_mul(normed, query_grad_low)
    grad_query_bias = jnp.sum(query_grad_low.astype(jnp.float32), axis=0)
    grad_key_weight = outer_mul(normed, key_grad_low)
    grad_value_weight = outer_mul(normed, value_grad_low)
    grad_value_bias = jnp.sum(value_grad_low.astype(jnp.float32), axis=0)
    grad_normed = (
        back_mul(query_grad_low, query_weight)
        + back_mul(key_grad_low, key_weight)
        + back_mul(value_grad_low, value_weight)
    )
    unused, first_pull = jax.vjp(
        layer_norm, start_vals, norm_gain.astype(jnp.float32), norm_shift.astype(jnp.float32)
    )
    grad_start, grad_norm_gain, grad_norm_shift = first_pull(grad_normed)
    input_grad = grad_residual + grad_start
    grads = (
        grad_norm_gain,
        grad_norm_shift,
        grad_query_weight,
        grad_query_bias,
        grad_key_weight,
        grad_value_weight,
        grad_value_bias,
        grad_output_weight,
        grad_output_bias,
        grad_second_gain,
        grad_second_shift,
        grad_up_weight,
        grad_up_bias,
        grad_down_weight,
        grad_down_bias,
    )
    return (input_grad, grads)


def body(
    tokens,
    norm_gain,
    norm_shift,
    query_weight,
    query_bias,
    key_weight,
    value_weight,
    value_bias,
    output_weight,
    output_bias,
    second_gain,
    second_shift,
    up_weight,
    up_bias,
    down_weight,
    down_bias,
    cotangent,
):
    micro_count = tokens.shape[0] // SEQ
    outputs = []
    input_grads = []
    summed = None
    for micro_index in range(micro_count):
        row_start = micro_index * SEQ
        gathered = (
            lax.all_gather(norm_gain, "dp", axis=0, tiled=True),
            lax.all_gather(norm_shift, "dp", axis=0, tiled=True),
            lax.all_gather(query_weight, "dp", axis=0, tiled=True),
            lax.all_gather(query_bias, "dp", axis=0, tiled=True),
            lax.all_gather(key_weight, "dp", axis=0, tiled=True),
            lax.all_gather(value_weight, "dp", axis=0, tiled=True),
            lax.all_gather(value_bias, "dp", axis=0, tiled=True),
            lax.all_gather(output_weight, "dp", axis=0, tiled=True),
            lax.all_gather(output_bias, "dp", axis=0, tiled=True),
            lax.all_gather(second_gain, "dp", axis=0, tiled=True),
            lax.all_gather(second_shift, "dp", axis=0, tiled=True),
            lax.all_gather(up_weight, "dp", axis=0, tiled=True),
            lax.all_gather(up_bias, "dp", axis=0, tiled=True),
            lax.all_gather(down_weight, "dp", axis=0, tiled=True),
            lax.all_gather(down_bias, "dp", axis=0, tiled=True),
        )
        stored, result = forward_pass(tokens[row_start : row_start + SEQ], gathered)
        weights_back = (
            lax.all_gather(norm_gain, "dp", axis=0, tiled=True),
            lax.all_gather(norm_shift, "dp", axis=0, tiled=True),
            lax.all_gather(query_weight, "dp", axis=0, tiled=True),
            lax.all_gather(query_bias, "dp", axis=0, tiled=True),
            lax.all_gather(key_weight, "dp", axis=0, tiled=True),
            lax.all_gather(value_weight, "dp", axis=0, tiled=True),
            lax.all_gather(value_bias, "dp", axis=0, tiled=True),
            lax.all_gather(output_weight, "dp", axis=0, tiled=True),
            lax.all_gather(output_bias, "dp", axis=0, tiled=True),
            lax.all_gather(second_gain, "dp", axis=0, tiled=True),
            lax.all_gather(second_shift, "dp", axis=0, tiled=True),
            lax.all_gather(up_weight, "dp", axis=0, tiled=True),
            lax.all_gather(up_bias, "dp", axis=0, tiled=True),
            lax.all_gather(down_weight, "dp", axis=0, tiled=True),
            lax.all_gather(down_bias, "dp", axis=0, tiled=True),
        )
        input_grad, grads = backward_pass(
            stored, weights_back, cotangent[row_start : row_start + SEQ]
        )
        summed = grads if summed is None else jax.tree.map(jnp.add, summed, grads)
        outputs.append(result)
        input_grads.append(input_grad)
    summed = (
        lax.psum_scatter(summed[0], "dp", scatter_dimension=0, tiled=True),
        lax.psum_scatter(summed[1], "dp", scatter_dimension=0, tiled=True),
        lax.psum_scatter(summed[2], "dp", scatter_dimension=0, tiled=True),
        lax.psum_scatter(summed[3], "dp", scatter_dimension=0, tiled=True),
        lax.psum_scatter(summed[4], "dp", scatter_dimension=0, tiled=True),
        lax.psum_scatter(summed[5], "dp", scatter_dimension=0, tiled=True),
        lax.psum_scatter(summed[6], "dp", scatter_dimension=0, tiled=True),
        lax.psum_scatter(summed[7], "dp", scatter_dimension=0, tiled=True),
        lax.psum_scatter(summed[8], "dp", scatter_dimension=0, tiled=True),
        lax.psum_scatter(summed[9], "dp", scatter_dimension=0, tiled=True),
        lax.psum_scatter(summed[10], "dp", scatter_dimension=0, tiled=True),
        lax.psum_scatter(summed[11], "dp", scatter_dimension=0, tiled=True),
        lax.psum_scatter(summed[12], "dp", scatter_dimension=0, tiled=True),
        lax.psum_scatter(summed[13], "dp", scatter_dimension=0, tiled=True),
        lax.psum_scatter(summed[14], "dp", scatter_dimension=0, tiled=True),
    )
    return (
        jnp.concatenate(outputs, axis=0),
        jnp.concatenate(input_grads, axis=0),
        summed[0],
        summed[1],
        summed[2],
        summed[3],
        summed[4],
        summed[5],
        summed[6],
        summed[7],
        summed[8],
        summed[9],
        summed[10],
        summed[11],
        summed[12],
        summed[13],
        summed[14],
    )


def solution(mesh):
    return jax.shard_map(
        body,
        mesh=mesh,
        in_specs=(
            P("dp", None),
            P("dp"),
            P("dp"),
            P("dp", None),
            P("dp"),
            P("dp", None),
            P("dp", None),
            P("dp"),
            P("dp", None),
            P("dp"),
            P("dp"),
            P("dp"),
            P("dp", None),
            P("dp"),
            P("dp", None),
            P("dp"),
            P("dp", None),
        ),
        out_specs=(
            P("dp", None),
            P("dp", None),
            P("dp"),
            P("dp"),
            P("dp", None),
            P("dp"),
            P("dp", None),
            P("dp", None),
            P("dp"),
            P("dp", None),
            P("dp"),
            P("dp"),
            P("dp"),
            P("dp", None),
            P("dp"),
            P("dp", None),
            P("dp"),
        ),
        check_vma=False,
    )
```

profile of v0, /device:TPU:0, one launch (start us, length us, event | category | flops | bytes accessed | tf_op | source)
XLA Modules:
  0.0 1284.0 jit_solution(15782227619437266066)
XLA Ops:
  18.9 42.6 %all-reduce.23 = (bf16[768]{0:T(1024)(128)(2,1)S(1)}, bf16[768]{0:T(1024)(128)(2,1)S(1)}, bf16[768]{0:T(1024)(128)(2,1)S(1)}, bf16[768]{0:T(1024)(128)(2,1)S(1)}...) all-reduce(bf16[768]{0:T(1024)(128)(2,1)S(1)} %dynamic-update-slice, ...), channel_id=1, replica_groups=mesh['dp'=32] {'dp'}, use_global_device_ids=true, to_apply=%add.6 | all-reduce | flops 9216 | bytes 36864
  74.8 49.2 %all-gather.7.cloned.1.call-done = bf16[768,768]{1,0:T(8,128)(2,1)} async-done(((bf16[24,768]{1,0:T(8,128)(2,1)}), bf16[768,768]{1,0:T(8,128)(2,1)}) %all-gather.7.cloned.1.call-update) | async-done | bytes 1179664 | tf_op jit(solution)/shard_map/all_gather | solution.py:315
  136.2 43.7 %all-gather.9.cloned.1.call-done = bf16[768,768]{1,0:T(8,128)(2,1)} async-done(((bf16[24,768]{1,0:T(8,128)(2,1)}), bf16[768,768]{1,0:T(8,128)(2,1)}) %all-gather.9.cloned.1.call-update) | async-done | bytes 1179664 | tf_op jit(solution)/shard_map/all_gather | solution.py:312
  189.4 15.7 %fusion = (f32[12,512]{1,0:T(8,128)S(1)}, f32[12,512,1024]{2,1,0:T(8,128)}) fusion(pred[512,1024]{1,0:T(8,128)(4,1)} %iota_compare_fusion, bf16[512,12,64]{0,2,1:T(8,128)(2,1)} %bitcast.176, bf16[1024,12,64]{0,2,1:T(8,128)(2,1)} %bitcast.174), kind=kOutput, calls=%fused_computation.10 | convolution fusion | flops 824174592 | bytes 28073984 | tf_op jit(solution)/shard_map/qhd,khd->hqk/dot_general | solution.py:52
  221.0 12.1 fusion.53
  261.1 39.9 %all-gather.15.cloned.1.call-done = bf16[768,3072]{1,0:T(8,128)(2,1)} async-done(((bf16[24,3072]{1,0:T(8,128)(2,1)}), bf16[768,3072]{1,0:T(8,128)(2,1)}) %all-gather.15.cloned.1.call-update) | async-done | bytes 4718608 | tf_op jit(solution)/shard_map/all_gather | solution.py:321
  311.6 54.7 %all-gather.17.cloned.1.call-done = bf16[3072,768]{1,0:T(8,128)(2,1)} async-done(((bf16[96,768]{1,0:T(8,128)(2,1)}), bf16[3072,768]{1,0:T(8,128)(2,1)}) %all-gather.17.cloned.1.call-update) | async-done | bytes 4718608 | tf_op jit(solution)/shard_map/all_gather | solution.py:323
  366.3 17.4 %convert_reduce_fusion.1 = (f32[3072]{0:T(1024)}, bf16[1024,3072]{1,0:T(8,128)(2,1)S(1)}) fusion(f32[1024,3072]{1,0:T(8,128)} %fusion.92, f32[3072]{0:T(1024)S(1)} %convert_element_type.232, bf16[3072,768]{1,0:T(8,128)(2,1)} %all-gather.17.cloned.1.call-done, bf16[2048,768]{1,0:T(8,128)(2,1)} %param.57), kind=kOutput, calls=%fused_computation.33 | convolution fusion | flops 4904186880 | bytes 25190400 | tf_op jit(solution)/shard_map/dot_general | solution.py:34
  418.9 27.5 %multiply_reduce_fusion.1 = (f32[12,512]{1,0:T(8,128)}, f32[12,512]{1,0:T(8,128)S(1)}, f32[12,512,1024]{2,1,0:T(8,128)}) fusion(f32[12,512,1024]{2,1,0:T(8,128)} %get-tuple-element.218, f32[12,512]{1,0:T(8,128)S(1)} %log_add_fusion.2, pred[512,1024]{1,0:T(8,128)(4,1)} %iota_compare_fusion, f32[12,512,1024]{2,1,0:T(8,128)} %fusion.111, ...), kind=kOutput, calls=%fused_computation.3 | convolution fusion | flops 855625728 | bytes 78454784 | tf_op jit(solution)/shard_map/qhd,khd->hqk/dot_general | solution.py:104
  487.0 15.5 %convert_reduce_fusion = (f32[3072]{0:T(1024)}, bf16[1024,3072]{1,0:T(8,128)(2,1)S(1)}) fusion(f32[1024,3072]{1,0:T(8,128)} %fusion.93, f32[3072]{0:T(1024)S(1)} %convert_element_type.232, bf16[3072,768]{1,0:T(8,128)(2,1)} %all-gather.17.cloned.1.call-done, bf16[2048,768]{1,0:T(8,128)(2,1)S(1)} %copy-done.23), kind=kOutput, calls=%fused_computation.32 | convolution fusion | flops 4904186880 | bytes 25190400 | tf_op jit(solution)/shard_map/dot_general | solution.py:34
  531.0 13.8 %convert_reduce_fusion.9 = (f32[12,64]{1,0:T(8,128)}, bf16[1024,12,64]{0,2,1:T(8,128)(2,1)}) fusion(bf16[512,12,64]{0,2,1:T(8,128)(2,1)S(1)} %bitcast.185, f32[12,512,1024]{2,1,0:T(8,128)} %get-tuple-element.218, f32[12,512]{1,0:T(8,128)S(1)} %log_add_fusion.2, pred[512,1024]{1,0:T(8,128)(4,1)S(1)} %copy-done.10, f32[512,12,64]{0,2,1:T(8,128)S(1)} %copy-done.131), kind=kOutput, calls=%fused_computation.107 | convolution fusion | flops 833617152 | bytes 29649920 | tf_op jit(solution)/shard_map/hqk,qhd->khd/dot_general | solution.py:128
  549.0 22.4 %multiply_reduce_fusion = (f32[12,512]{1,0:T(8,128)}, f32[12,512,1024]{2,1,0:T(8,128)}) fusion(f32[12,512,1024]{2,1,0:T(8,128)} %fusion.111, f32[12,512]{1,0:T(8,128)S(1)} %log_add_fusion, pred[512,1024]{1,0:T(8,128)(4,1)S(1)} %copy-done.10, bf16[512,12,64]{0,2,1:T(8,128)(2,1)S(1)} %bitcast.194, bf16[1024,12,64]{0,2,1:T(8,128)(2,1)S(1)} %bitcast.187), kind=kOutput, calls=%fused_computation.1 | convolution fusion | flops 836757504 | bytes 53264384 | tf_op jit(solution)/shard_map/qhd,khd->hqk/dot_general | solution.py:104
  571.4 14.3 %convert_reduce_fusion.8 = (f32[12,64]{1,0:T(8,128)}, bf16[1024,12,64]{0,2,1:T(8,128)(2,1)}) fusion(bf16[512,12,64]{0,2,1:T(8,128)(2,1)S(1)} %bitcast.195, f32[12,512,1024]{2,1,0:T(8,128)} %fusion.111, f32[12,512]{1,0:T(8,128)S(1)} %log_add_fusion, pred[512,1024]{1,0:T(8,128)(4,1)S(1)} %copy-done.10, f32[512,12,64]{0,2,1:T(8,128)} %convolution_bitcast_fusion), kind=kOutput, calls=%fused_computation.106 | convolution fusion | flops 833617152 | bytes 29649920 | tf_op jit(solution)/shard_map/hqk,qhd->khd/dot_general | solution.py:128
  585.8 21.5 %multiply_convert_fusion.2 = (bf16[12,512,512]{1,2,0:T(8,128)(2,1)S(1)}, bf16[12,512,512]{1,2,0:T(8,128)(2,1)}) fusion(f32[12,512,512]{1,2,0:T(8,128)} %get-tuple-element.232, f32[12,512,512]{1,2,0:T(8,128)} %fusion.110, f32[12,512]{1,0:T(8,128)S(1)} %get-tuple-element.231, f32[12,512]{1,0:T(8,128)S(1)} %log_add_fusion.1, ...), kind=kLoop, calls=%fused_computation.34 | loop fusion | flops 37748736 | bytes 63275008 | tf_op jit(solution)/shard_map/convert_element_type | solution.py:111
  614.4 42.7 %multiply_convert_fusion = (bf16[12,512,1024]{2,1,0:T(8,128)(2,1)}, bf16[12,512,1024]{2,1,0:T(8,128)(2,1)}) fusion(f32[12,512,1024]{2,1,0:T(8,128)} %get-tuple-element.230, f32[12,512,1024]{2,1,0:T(8,128)} %fusion.111, f32[12,512]{1,0:T(8,128)S(1)} %copy-done.86, f32[12,512]{1,0:T(8,128)S(1)} %log_add_fusion, pred[512,1024]{1,0:T(8,128)(4,1)} %iota_compare_fusion, ...), kind=kLoop, calls=%fused_computation | loop fusion | flops 75497472 | bytes 126451712 | tf_op jit(solution)/shard_map/convert_element_type | solution.py:111
  723.4 13.3 %fusion.58 = f32[3072,768]{1,0:T(8,128)} fusion(bf16[2048,768]{1,0:T(8,128)(2,1)} %param.57, f32[1024,3072]{1,0:T(8,128)} %fusion.92, f32[3072]{0:T(1024)S(1)} %copy-done.111), kind=kOutput, calls=%fused_computation.158 | convolution fusion | flops 4863295488 | bytes 23605248 | tf_op jit(solution)/shard_map/dot_general | solution.py:28
  736.8 14.8 %convolution_add_fusion = f32[3072,768]{1,0:T(8,128)} fusion(f32[3072,768]{1,0:T(8,128)} %fusion.58, bf16[2048,768]{1,0:T(8,128)(2,1)} %param.57, f32[1024,3072]{1,0:T(8,128)} %fusion.93, f32[3072]{0:T(1024)S(1)} %copy-done.111), kind=kOutput, calls=%fused_computation.51 | convolution fusion | flops 4865654784 | bytes 33042432 | tf_op jit(solution)/shard_map/dot_general | solution.py:28
  790.7 40.7 %all-reduce.22 = (f32[768]{0:T(1024)S(1)}, f32[768]{0:T(1024)S(1)}, f32[768]{0:T(1024)S(1)}, f32[768]{0:T(1024)S(1)}, f32[768]{0:T(1024)S(1)}, /*index=5*/f32[76...) all-reduce(f32[768]{0:T(1024)S(1)} %add.442, ...), channel_id=2, replica_groups=mesh['dp'=32] {'dp'}, use_global_device_ids=true, to_apply=%region_30.31.clone | all-reduce | flops 9216 | bytes 73728
  836.6 13.0 %add_convert_fusion.4 = bf16[1024,768]{1,0:T(8,128)(2,1)S(1)} fusion(f32[1024,768]{1,0:T(8,128)} %copy-done.11, bf16[3072,768]{1,0:T(8,128)(2,1)} %all-gather.17.cloned.1.call-done, f32[768]{0:T(1024)S(1)} %convert_element_type.234, f32[1024,3072]{1,0:T(8,128)} %fusion.92, f32[3072]{0:T(1024)S(1)} %copy-done.111), kind=kOutput, calls=%fused_computation.121 | convolution fusion | flops 4865654784 | bytes 22035456 | tf_op jit(solution)/shard_map/dot_general | solution.py:24
  849.7 12.3 add_convert_fusion
  872.2 17.3 %reduce-scatter.7.cloned.1.call-done = f32[24,768]{1,0:T(8,128)} async-done(((f32[768,768]{1,0:T(8,128)}), f32[24,768]{1,0:T(8,128)}) %reduce-scatter.7.cloned.1.call-update) | async-done | bytes 73744 | tf_op jit(solution)/shard_map/reduce_scatter | solution.py:353
  889.5 104.7 %reduce-scatter.9.cloned.1.call-done = f32[24,768]{1,0:T(8,128)} async-done(((f32[768,768]{1,0:T(8,128)}), f32[24,768]{1,0:T(8,128)}) %reduce-scatter.9.cloned.1.call-update) | async-done | bytes 73744 | tf_op jit(solution)/shard_map/reduce_scatter | solution.py:355
  994.2 141.1 %reduce-scatter.17.cloned.1.call-done = f32[96,768]{1,0:T(8,128)} async-done(((f32[3072,768]{1,0:T(8,128)}), f32[96,768]{1,0:T(8,128)}) %reduce-scatter.17.cloned.1.call-update) | async-done | bytes 294928 | tf_op jit(solution)/shard_map/reduce_scatter | solution.py:364
  1135.3 141.7 %reduce-scatter.15.cloned.1.call-done = f32[24,3072]{1,0:T(8,128)} async-done(((f32[768,3072]{1,0:T(8,128)}), f32[24,3072]{1,0:T(8,128)}) %reduce-scatter.15.cloned.1.call-update) | async-done | bytes 294928 | tf_op jit(solution)/shard_map/reduce_scatter | solution.py:362
  (469 shorter events, 336.0 us)
Async XLA Ops:
  7.2 62.3 %all-gather.11.cloned.1.call-start = ((), (), s32[]{:S(2)}) async-start(), calls=%async_computation.8 | async-start | bytes 1216512 | tf_op jit(solution)/shard_map/all_gather | solution.py:314
  7.9 116.1 %all-gather.7.cloned.1.call-start = ((), (), s32[]{:S(2)}) async-start(), calls=%async_computation.6 | async-start | bytes 1216512 | tf_op jit(solution)/shard_map/all_gather | solution.py:315
  8.7 171.2 %all-gather.9.cloned.1.call-start = ((), (), s32[]{:S(2)}) async-start(), calls=%async_computation.7 | async-start | bytes 1216512 | tf_op jit(solution)/shard_map/all_gather | solution.py:312
  9.4 226.3 %all-gather.13.cloned.1.call-start = ((), (), s32[]{:S(2)}) async-start(), calls=%async_computation.9 | async-start | bytes 1216512 | tf_op jit(solution)/shard_map/all_gather | solution.py:317
  10.0 291.0 %all-gather.15.cloned.1.call-start = ((), (), s32[]{:S(2)}) async-start(), calls=%async_computation.10 | async-start | bytes 4866048 | tf_op jit(solution)/shard_map/all_gather | solution.py:321
  10.6 355.7 %all-gather.17.cloned.1.call-start = ((), (), s32[]{:S(2)}) async-start(), calls=%async_computation.11 | async-start | bytes 4866048 | tf_op jit(solution)/shard_map/all_gather | solution.py:323
  11.2 861.1 %reduce-scatter.13.cloned.1.call-start = ((), (), s32[]{:S(2)}) async-start(), calls=%async_computation.15 | async-start | bytes 2433024 | tf_op jit(solution)/shard_map/reduce_scatter | solution.py:358
  61.5 179.8 %copy-start.88 = (f32[768]{0:T(1024)}, f32[768]{0:T(1024)S(1)}, u32[]{:S(2)}) copy-start(f32[768]{0:T(1024)S(1)} %convert_element_type.217) | copy-start | bytes 9220
  61.5 452.0 %copy-start.69 = (f32[768]{0:T(1024)}, f32[768]{0:T(1024)S(1)}, u32[]{:S(2)}) copy-start(f32[768]{0:T(1024)S(1)} %convert_element_type.229) | copy-start | bytes 9220
  61.6 179.8 %copy-start.108 = (f32[768]{0:T(1024)}, f32[768]{0:T(1024)S(1)}, u32[]{:S(2)}) copy-start(f32[768]{0:T(1024)S(1)} %convert_element_type.218) | copy-start | bytes 9220
  61.6 416.7 %copy-start.71 = (f32[768]{0:T(1024)}, f32[768]{0:T(1024)S(1)}, u32[]{:S(2)}) copy-start(f32[768]{0:T(1024)S(1)} %convert_element_type.230) | copy-start | bytes 9220
  61.6 174.1 %copy-start.120 = (f32[768]{0:T(1024)}, f32[768]{0:T(1024)S(1)}, u32[]{:S(2)}) copy-start(f32[768]{0:T(1024)S(1)} %convert_element_type.228) | copy-start | bytes 9220
  64.0 177.3 %copy-start.90 = (f32[1024]{0:T(1024)}, f32[1024]{0:T(1024)S(1)}, u32[]{:S(2)}) copy-start(f32[1024]{0:T(1024)S(1)} %get-tuple-element.242) | copy-start | bytes 12292
  66.5 174.9 %copy-start.94 = (f32[1024]{0:T(1024)}, f32[1024]{0:T(1024)S(1)}, u32[]{:S(2)}) copy-start(f32[1024]{0:T(1024)S(1)} %fusion.71) | copy-start | bytes 12292
  66.5 420.6 %copy-start.110 = (f32[3072]{0:T(1024)}, f32[3072]{0:T(1024)S(1)}, u32[]{:S(2)}) copy-start(f32[3072]{0:T(1024)S(1)} %convert_element_type.232) | copy-start | bytes 36868
  189.4 215.2 %copy-start.77 = (f32[12,512]{1,0:T(8,128)}, f32[12,512]{1,0:T(8,128)S(1)}, u32[]{:S(2)}) copy-start(f32[12,512]{1,0:T(8,128)S(1)} %log_add_fusion.3) | copy-start | bytes 73732
  239.1 150.5 %copy-start.73 = (f32[1024]{0:T(1024)}, f32[1024]{0:T(1024)S(1)}, u32[]{:S(2)}) copy-start(f32[1024]{0:T(1024)S(1)} %broadcast_multiply_fusion.2) | copy-start | bytes 12292
  241.4 148.3 %copy-start.79 = (f32[1024]{0:T(1024)}, f32[1024]{0:T(1024)S(1)}, u32[]{:S(2)}) copy-start(f32[1024]{0:T(1024)S(1)} %fusion.70) | copy-start | bytes 12292
  547.7 324.6 %reduce-scatter.11.cloned.1.call-start = ((), (), s32[]{:S(2)}) async-start(), calls=%async_computation.14 | async-start | bytes 2433024 | tf_op jit(solution)/shard_map/reduce_scatter | solution.py:356
  607.2 56.9 %copy-start.1 = (bf16[12,512,512]{1,2,0:T(8,128)(2,1)}, bf16[12,512,512]{1,2,0:T(8,128)(2,1)S(1)}, u32[]{:S(2)}) copy-start(bf16[12,512,512]{1,2,0:T(8,128)(2,1)S(1)} %get-tuple-element.215) | copy-start | bytes 18874372
  687.5 202.0 %reduce-scatter.7.cloned.1.call-start = ((), (), s32[]{:S(2)}) async-start(), calls=%async_computation.12 | async-start | bytes 2433024 | tf_op jit(solution)/shard_map/reduce_scatter | solution.py:353
  717.6 276.6 %reduce-scatter.9.cloned.1.call-start = ((), (), s32[]{:S(2)}) async-start(), calls=%async_computation.13 | async-start | bytes 2433024 | tf_op jit(solution)/shard_map/reduce_scatter | solution.py:355
  736.7 398.6 %reduce-scatter.17.cloned.1.call-start = ((), (), s32[]{:S(2)}) async-start(), calls=%async_computation.17 | async-start | bytes 9732096 | tf_op jit(solution)/shard_map/reduce_scatter | solution.py:364
  751.7 525.3 %reduce-scatter.15.cloned.1.call-start = ((), (), s32[]{:S(2)}) async-start(), calls=%async_computation.16 | async-start | bytes 9732096 | tf_op jit(solution)/shard_map/reduce_scatter | solution.py:362
  (133 other events, 897.8 us)
Sparse Core Ops, SparseCore 0:
  10.9 56.9 all-gather.10
  70.8 53.1 all-gather.6
  126.9 52.9 all-gather.8
  182.7 52.9 all-gather.12
  238.4 62.5 all-gather.14
  303.8 62.4 all-gather.16
  547.8 97.8 reduce-scatter.12
  687.6 97.9 reduce-scatter.10
  791.5 97.9 reduce-scatter.6
  896.0 98.0 reduce-scatter.8
  1000.7 134.6 reduce-scatter.16
  1142.6 134.3 reduce-scatter.14
where the time goes:
time: 1290 us; the launch traced here: 1280 us
  waiting for transfers between devices  597 us (46%)
  matrix products  425 us (33%)
  other arithmetic  121 us (9%)
  blocking collectives  83.3 us (6%)
  local copies, waits for them, and re-layouts  41 us (3%)
  between operations  16.2 us (1%)
    reduce_scatter x1, waiting for transfers between devices, body(): lax.psum_scatter(summed[11], 'dp', scatter_dimension=0, tiled=True)  142 us
    reduce_scatter x1, waiting for transfers between devices, body(): lax.psum_scatter(summed[13], 'dp', scatter_dimension=0, tiled=True)  141 us
    reduce_scatter x1, waiting for transfers between devices, body(): lax.psum_scatter(summed[4], 'dp', scatter_dimension=0, tiled=True)  105 us
    unnamed x2, blocking collectives  83.3 us
    dot_general x12, matrix products, outer_mul(): lax.dot_general(left, right, (((0,), (0,)), ((), ())), preferred_element_...  74.5 us
    dot_general x4, matrix products, attention_backward(): jnp.einsum('qhd,khd->hqk', grad_heads[row_start:row_end], value_heads[:ro...  68.3 us
    dot_general x12, matrix products, back_mul(): lax.dot_general(left, right, (((1,), (1,)), ((), ())), preferred_element_...  65 us
    dot_general x12, matrix products, dense_mul(): return jnp.dot(left, right, preferred_element_type=jnp.float32)  64.7 us
  transfers between devices with their start and end apart: 12, of which 9 were waited for; matrix products, arithmetic and copies ran while one was open for 30% of the time, Pallas kernels for 0%

commit v1 on v0

v1 whole, which is shorter than its diff:
```python
import functools

import jax
import jax.numpy as jnp
from jax import lax
from jax.experimental import pallas as pl
from jax.experimental.pallas import tpu as pltpu
from jax.sharding import PartitionSpec as P

HD = 64
SEQ = 1024
LANES = 128
QUERY_BLOCK = 256
F32 = jnp.float32
BF16 = jnp.bfloat16
EPSILON = 1e-05
GELU_SCALE = 0.7978845608028654
GELU_CUBIC = 0.044715


def dot_nn(left, right):
    return lax.dot_general(left, right, (((1,), (0,)), ((), ())), preferred_element_type=F32)


def dot_nt(left, right):
    return lax.dot_general(left, right, (((1,), (1,)), ((), ())), preferred_element_type=F32)


def dot_tn(left, right):
    return lax.dot_general(left, right, (((0,), (0,)), ((), ())), preferred_element_type=F32)


def normalise(values):
    center = values - jnp.mean(values, axis=-1, keepdims=True)
    rstd = lax.rsqrt(jnp.mean(center * center, axis=-1, keepdims=True) + EPSILON)
    return center * rstd, rstd


def whole(shape):
    return pl.BlockSpec(shape, lambda *_: (0,) * len(shape), pipeline_mode=pl.Buffered(1))


def rows(block, width):
    return pl.BlockSpec((block, width), lambda i: (i, 0))


def project_kernel(x_ref, vec_ref, wq_ref, wk_ref, wv_ref, h_ref, q_ref, k_ref, v_ref):
    normed, _ = normalise(x_ref[...].astype(F32))
    h = (normed * vec_ref[0:1, :] + vec_ref[1:2, :]).astype(BF16)
    h_ref[...] = h
    q = (dot_nn(h, wq_ref[...]) + vec_ref[2:3, :]).astype(BF16)
    q_ref[...] = (q.astype(F32) * HD**-0.5).astype(BF16)
    k_ref[...] = dot_nn(h, wk_ref[...]).astype(BF16)
    v_ref[...] = (dot_nn(h, wv_ref[...]) + vec_ref[3:4, :]).astype(BF16)


def project(tokens, vecs, wq, wk, wv):
    count, width = tokens.shape
    block = 512
    out = jax.ShapeDtypeStruct((count, width), BF16)
    return pl.pallas_call(
        project_kernel,
        grid=(count // block,),
        in_specs=[rows(block, width), whole(vecs.shape)] + [whole((width, width))] * 3,
        out_specs=[rows(block, width)] * 4,
        out_shape=[out] * 4,
        compiler_params=pltpu.CompilerParams(vmem_limit_bytes=48 * 2**20),
        cost_estimate=pl.CostEstimate(
            flops=6 * count * width * width,
            bytes_accessed=10 * count * width + 6 * width * width,
            transcendentals=0,
        ),
        name="project",
    )(tokens, vecs, wq, wk, wv)


def head_only(values, head):
    lane = lax.broadcasted_iota(jnp.int32, values.shape, 1)
    keep = (lane < HD) if head == 0 else (lane >= HD)
    return jnp.where(keep, values, jnp.zeros_like(values))


def causal_t(scores_t):
    key = lax.broadcasted_iota(jnp.int32, scores_t.shape, 0)
    query = lax.broadcasted_iota(jnp.int32, scores_t.shape, 1)
    return key <= query


def attend_kernel(q_ref, k_ref, v_ref, o_ref, lse_ref, out_t):
    seq_len = q_ref.shape[0]
    k = k_ref[...]
    v_t = v_ref[...].astype(F32).T.astype(BF16)
    for head in range(2):
        q = head_only(q_ref[...], head)
        v_head = v_t[head * HD : (head + 1) * HD, :]
        for start in range(0, seq_len, QUERY_BLOCK):
            end = start + QUERY_BLOCK
            q_part = q[start:end]
            diag = dot_nt(k[start:end], q_part)
            diag = jnp.where(causal_t(diag), diag, -jnp.inf)
            peak = jnp.max(diag, axis=0, keepdims=True)
            if start:
                full = dot_nt(k[:start], q_part)
                peak = jnp.maximum(peak, jnp.max(full, axis=0, keepdims=True))
            p_diag = jnp.exp(diag - peak)
            total = jnp.sum(p_diag, axis=0, keepdims=True)
            mixed = dot_nn(v_head[:, start:end], p_diag.astype(BF16))
            if start:
                p_full = jnp.exp(full - peak)
                total = total + jnp.sum(p_full, axis=0, keepdims=True)
                mixed = mixed + dot_nn(v_head[:, :start], p_full.astype(BF16))
            out_t[head * HD : (head + 1) * HD, start:end] = mixed * (1.0 / total)
            lse_ref[0, 0, head : head + 1, start:end] = peak + jnp.log(total)
    o_ref[...] = out_t[...].T.astype(BF16)


def attend(q, k, v):
    count, width = q.shape
    seqs, pairs = count // SEQ, width // LANES
    block = pl.BlockSpec((SEQ, LANES), lambda s, p: (s, p))
    return pl.pallas_call(
        attend_kernel,
        grid=(seqs, pairs),
        in_specs=[block] * 3,
        out_specs=[block, pl.BlockSpec((1, 1, 2, SEQ), lambda s, p: (s, p, 0, 0))],
        out_shape=[
            jax.ShapeDtypeStruct((count, width), BF16),
            jax.ShapeDtypeStruct((seqs, pairs, 2, SEQ), F32),
        ],
        scratch_shapes=[pltpu.VMEM((LANES, SEQ), F32)],
        compiler_params=pltpu.CompilerParams(vmem_limit_bytes=48 * 2**20),
        cost_estimate=pl.CostEstimate(
            flops=4 * count * SEQ * width,
            bytes_accessed=8 * count * width,
            transcendentals=count * SEQ * width // HD,
        ),
        name="attend",
    )(q, k, v)


def attend_back_kernel(
    q_ref, k_ref, v_ref, do_ref, lse_ref, dq_ref, dk_ref, dv_ref, sums_ref, dq_t, dk_acc, dv_acc
):
    seq_len = q_ref.shape[0]
    k = k_ref[...]
    v = v_ref[...]
    k_t = k.astype(F32).T.astype(BF16)
    dk_acc[...] = jnp.zeros_like(dk_acc)
    dv_acc[...] = jnp.zeros_like(dv_acc)
    for head in range(2):
        q = head_only(q_ref[...], head)
        do = head_only(do_ref[...], head)
        k_head = k_t[head * HD : (head + 1) * HD, :]
        for start in range(0, seq_len, QUERY_BLOCK):
            end = start + QUERY_BLOCK
            q_part = q[start:end]
            do_part = do[start:end]
            lse = lse_ref[0, 0, head : head + 1, start:end]
            scores = dot_nt(k[start:end], q_part)
            p_diag = jnp.exp(jnp.where(causal_t(scores), scores, -jnp.inf) - lse)
            dp_diag = dot_nt(v[start:end], do_part)
            inner = jnp.sum(p_diag * dp_diag, axis=0, keepdims=True)
            if start:
                p_full = jnp.exp(dot_nt(k[:start], q_part) - lse)
                dp_full = dot_nt(v[:start], do_part)
                inner = inner + jnp.sum(p_full * dp_full, axis=0, keepdims=True)
                ds_full = (p_full * (dp_full - inner)).astype(BF16)
                dv_acc[:start, :] += dot_nn(p_full.astype(BF16), do_part)
                dk_acc[:start, :] += dot_nn(ds_full, q_part)
            ds_diag = (p_diag * (dp_diag - inner)).astype(BF16)
            dv_acc[start:end, :] += dot_nn(p_diag.astype(BF16), do_part)
            dk_acc[start:end, :] += dot_nn(ds_diag, q_part)
            dq = dot_nn(k_head[:, start:end], ds_diag)
            if start:
                dq = dq + dot_nn(k_head[:, :start], ds_full)
            dq_t[head * HD : (head + 1) * HD, start:end] = dq
    dq = (dq_t[...].T * HD**-0.5).astype(BF16)
    dv = dv_acc[...].astype(BF16)
    dq_ref[...] = dq
    dk_ref[...] = dk_acc[...].astype(BF16)
    dv_ref[...] = dv
    sums_ref[0, 0:1, :] = jnp.sum(dq.astype(F32), axis=0, keepdims=True)
    sums_ref[0, 1:2, :] = jnp.sum(dv.astype(F32), axis=0, keepdims=True)


def attend_back(q, k, v, d_attn, lse):
    count, width = q.shape
    seqs, pairs = count // SEQ, width // LANES
    block = pl.BlockSpec((SEQ, LANES), lambda s, p: (s, p))
    out = jax.ShapeDtypeStruct((count, width), BF16)
    return pl.pallas_call(
        attend_back_kernel,
        grid=(seqs, pairs),
        in_specs=[block] * 4 + [pl.BlockSpec((1, 1, 2, SEQ), lambda s, p: (s, p, 0, 0))],
        out_specs=[block] * 3 + [pl.BlockSpec((1, 2, LANES), lambda s, p: (s, 0, p))],
        out_shape=[out] * 3 + [jax.ShapeDtypeStruct((seqs, 2, width), F32)],
        scratch_shapes=[
            pltpu.VMEM((LANES, SEQ), F32),
            pltpu.VMEM((SEQ, LANES), F32),
            pltpu.VMEM((SEQ, LANES), F32),
        ],
        compiler_params=pltpu.CompilerParams(vmem_limit_bytes=48 * 2**20),
        cost_estimate=pl.CostEstimate(
            flops=10 * count * SEQ * width,
            bytes_accessed=14 * count * width,
            transcendentals=count * SEQ * width // HD,
        ),
        name="attend_back",
    )(q, k, v, d_attn, lse)


def feed_kernel(
    x_ref, a_ref, dy_ref, vec_ref, ub_ref, wo_hbm, wu_hbm, wd_hbm,
    mixed_ref, dr_ref, da_ref, gvec_ref, gub_ref, go_hbm, gu_hbm, gd_hbm,
    wo, wu, wd, acc_o, acc_u, acc_d, sems,
):
    step = pl.program_id(0)
    width = x_ref.shape[1]
    pieces = ((wo_hbm, wo, acc_o, go_hbm), (wu_hbm, wu, acc_u, gu_hbm), (wd_hbm, wd, acc_d, gd_hbm))

    @pl.when(step == 0)
    def _():
        for place, (source, held, _, _) in enumerate(pieces):
            pltpu.make_async_copy(source, held, sems.at[place]).start()
        for _, _, total, _ in pieces:
            total[...] = jnp.zeros_like(total)
        gvec_ref[...] = jnp.zeros_like(gvec_ref)
        gub_ref[...] = jnp.zeros_like(gub_ref)
        for place, (source, held, _, _) in enumerate(pieces):
            pltpu.make_async_copy(source, held, sems.at[place]).wait()

    attn = a_ref[...]
    dy = dy_ref[...]
    dy_wide = dy.astype(F32)
    resid = x_ref[...].astype(F32) + dot_nn(attn, wo[...]) + vec_ref[4:5, :]
    normed, rstd = normalise(resid)
    gain = vec_ref[5:6, :]
    h2 = (normed * gain + vec_ref[6:7, :]).astype(BF16)

    def chunk(index, carry):
        mixed, dh2 = carry
        cols = pl.ds(pl.multiple_of(index * width, width), width)
        u = dot_nn(h2, wu[cols, :]) + ub_ref[:, cols]
        d_act = dot_nt(dy, wd[cols, :])
        square = u * u
        tanh = jnp.tanh(GELU_SCALE * u * (1.0 + GELU_CUBIC * square))
        half = 0.5 + 0.5 * tanh
        act = (u * half).astype(BF16)
        slope = half + u * (0.5 - 0.5 * tanh * tanh) * (
            GELU_SCALE * (1.0 + 3.0 * GELU_CUBIC * square)
        )
        du = (d_act * slope).astype(BF16)
        gub_ref[:, cols] += jnp.sum(du.astype(F32), axis=0, keepdims=True)
        acc_d[cols, :] += dot_tn(act, dy)
        acc_u[cols, :] += dot_tn(h2, du)
        return (mixed + dot_nn(act, wd[cols, :]), dh2 + dot_nt(du, wu[cols, :]))

    mixed, dh2 = lax.fori_loop(
        0, wu.shape[0] // width, chunk, (resid + vec_ref[7:8, :], jnp.zeros_like(resid))
    )
    mixed_ref[...] = mixed.astype(BF16)
    g = dh2 * gain
    dr = dy_wide + rstd * (
        g
        - jnp.mean(g, axis=-1, keepdims=True)
        - normed * jnp.mean(g * normed, axis=-1, keepdims=True)
    )
    dr_ref[...] = dr
    da = dr.astype(BF16)
    da_ref[...] = dot_nt(da, wo[...]).astype(BF16)
    acc_o[...] += dot_tn(attn, da)
    gvec_ref[0:1, :] += jnp.sum(da.astype(F32), axis=0, keepdims=True)
    gvec_ref[1:2, :] += jnp.sum(dh2 * normed, axis=0, keepdims=True)
    gvec_ref[2:3, :] += jnp.sum(dh2, axis=0, keepdims=True)
    gvec_ref[3:4, :] += jnp.sum(dy_wide, axis=0, keepdims=True)

    @pl.when(step == pl.num_programs(0) - 1)
    def _():
        for place, (_, held, total, out) in enumerate(pieces):
            held[...] = total[...].astype(BF16)
            pltpu.make_async_copy(held, out, sems.at[place]).start()
        for place, (_, held, _, out) in enumerate(pieces):
            pltpu.make_async_copy(held, out, sems.at[place]).wait()


def feed(tokens, attn, cotangent, vecs, up_bias, wo, wu, wd):
    count, width = tokens.shape
    block = 512
    any_spec = pl.BlockSpec(memory_space=pl.ANY)
    weights = (wo, wu, wd)
    return pl.pallas_call(
        feed_kernel,
        grid=(count // block,),
        in_specs=[rows(block, width)] * 3 + [whole(vecs.shape), whole(up_bias.shape)] + [any_spec] * 3,
        out_specs=[rows(block, width)] * 3 + [whole((4, width)), whole(up_bias.shape)] + [any_spec] * 3,
        out_shape=[
            jax.ShapeDtypeStruct((count, width), BF16),
            jax.ShapeDtypeStruct((count, width), F32),
            jax.ShapeDtypeStruct((count, width), BF16),
            jax.ShapeDtypeStruct((4, width), F32),
            jax.ShapeDtypeStruct(up_bias.shape, F32),
        ] + [jax.ShapeDtypeStruct(w.shape, BF16) for w in weights],
        scratch_shapes=[pltpu.VMEM(w.shape, BF16) for w in weights]
        + [pltpu.VMEM(w.shape, F32) for w in weights]
        + [pltpu.SemaphoreType.DMA((3,))],
        compiler_params=pltpu.CompilerParams(vmem_limit_bytes=60 * 2**20),
        cost_estimate=pl.CostEstimate(
            flops=6 * count * sum(w.size for w in weights),
            bytes_accessed=14 * count * width + 4 * sum(w.size for w in weights),
            transcendentals=count * up_bias.size,
        ),
        name="feed",
    )(tokens, attn, cotangent, vecs, up_bias, wo, wu, wd)


def input_grad_kernel(
    x_ref, dr_ref, dq_ref, dk_ref, dv_ref, vec_ref, wq_ref, wk_ref, wv_ref, ig_ref, sums_ref
):
    @pl.when(pl.program_id(0) == 0)
    def _():
        sums_ref[...] = jnp.zeros_like(sums_ref)

    normed, rstd = normalise(x_ref[...].astype(F32))
    dh = (
        dot_nt(dq_ref[...], wq_ref[...])
        + dot_nt(dk_ref[...], wk_ref[...])
        + dot_nt(dv_ref[...], wv_ref[...])
    )
    g = dh * vec_ref[0:1, :]
    ig_ref[...] = dr_ref[...] + rstd * (
        g
        - jnp.mean(g, axis=-1, keepdims=True)
        - normed * jnp.mean(g * normed, axis=-1, keepdims=True)
    )
    sums_ref[0:1, :] += jnp.sum(dh * normed, axis=0, keepdims=True)
    sums_ref[1:2, :] += jnp.sum(dh, axis=0, keepdims=True)


def input_gradient(tokens, dr, dq, dk, dv, vecs, wq, wk, wv):
    count, width = tokens.shape
    block = 512
    return pl.pallas_call(
        input_grad_kernel,
        grid=(count // block,),
        in_specs=[rows(block, width)] * 5 + [whole(vecs.shape)] + [whole((width, width))] * 3,
        out_specs=[rows(block, width), whole((2, width))],
        out_shape=[
            jax.ShapeDtypeStruct((count, width), F32),
            jax.ShapeDtypeStruct((2, width), F32),
        ],
        compiler_params=pltpu.CompilerParams(vmem_limit_bytes=48 * 2**20),
        cost_estimate=pl.CostEstimate(
            flops=6 * count * width * width,
            bytes_accessed=16 * count * width + 6 * width * width,
            transcendentals=0,
        ),
        name="input_gradient",
    )(tokens, dr, dq, dk, dv, vecs, wq, wk, wv)


def body(
    tokens, norm_gain, norm_shift, query_weight, query_bias, key_weight, value_weight, value_bias,
    output_weight, output_bias, second_gain, second_shift, up_weight, up_bias, down_weight,
    down_bias, cotangent,
):
    width = tokens.shape[1]
    share = query_weight.shape[0]
    devices = width // share
    fan = up_weight.shape[1] // width

    small = jnp.concatenate(
        [norm_gain, norm_shift, query_bias, value_bias, output_bias, second_gain, second_shift, down_bias, up_bias]
    )
    small = jnp.pad(small, (0, width - small.shape[0]))[None]
    early = jnp.concatenate([query_weight, key_weight, value_weight, small])
    early = lax.all_gather(early, "dp", axis=0)
    up_tall = up_weight.reshape(share, fan, width).transpose(1, 0, 2).reshape(fan * share, width)
    late = jnp.concatenate([output_weight, down_weight, up_tall])
    late = lax.all_gather(late, "dp", axis=0)

    wq, wk, wv = (
        early[:, place * share : (place + 1) * share].reshape(width, width) for place in range(3)
    )
    small = early[:, 3 * share]
    vecs = (
        small[:, : 8 * share].reshape(devices, 8, share).transpose(1, 0, 2).reshape(8, width).astype(F32)
    )
    up_bias_all = small[:, 8 * share : (8 + fan) * share].reshape(1, fan * width).astype(F32)
    wo = late[:, :share].reshape(width, width)
    wd = late[:, share : (1 + fan) * share].reshape(fan * width, width)
    wu = (
        late[:, (1 + fan) * share :]
        .reshape(devices, fan, share, width)
        .transpose(1, 0, 2, 3)
        .reshape(fan * width, width)
    )

    h, q, k, v = project(tokens, vecs, wq, wk, wv)
    attn, lse = attend(q, k, v)
    mixed, dr, d_attn, vec_sums, up_bias_sum, g_wo, g_wu, g_wd = feed(
        tokens, attn, cotangent, vecs, up_bias_all, wo, wu, wd
    )
    late = jnp.concatenate(
        [
            g_wo.reshape(devices, share, width),
            g_wd.reshape(devices, fan * share, width),
            g_wu.reshape(fan, devices, share, width).transpose(1, 0, 2, 3).reshape(devices, fan * share, width),
        ],
        axis=1,
    )
    late = lax.psum_scatter(late, "dp", scatter_dimension=0)

    dq, dk, dv, bias_sums = attend_back(q, k, v, d_attn, lse)
    input_grad, norm_sums = input_gradient(tokens, dr, dq, dk, dv, vecs, wq, wk, wv)
    bias_sums = jnp.sum(bias_sums, axis=0)
    sums = jnp.concatenate([norm_sums, bias_sums, vec_sums])
    sums = sums.reshape(8, devices, share).transpose(1, 0, 2).reshape(devices, 8 * share)
    sums = jnp.concatenate([sums, up_bias_sum.reshape(devices, fan * share)], axis=1)
    sums = jnp.pad(sums, ((0, 0), (0, width - sums.shape[1])))
    early = jnp.concatenate(
        [dot_tn(h, part).astype(BF16).reshape(devices, share, width) for part in (dq, dk, dv)]
        + [sums.astype(BF16)[:, None]],
        axis=1,
    )
    early = lax.psum_scatter(early, "dp", scatter_dimension=0).astype(F32)
    late = late.astype(F32)
    g_wq, g_wk, g_wv = (early[place * share : (place + 1) * share] for place in range(3))
    sums = early[3 * share]
    vec_grads = [sums[place * share : (place + 1) * share] for place in range(8)]
    g_up_bias = sums[8 * share : (8 + fan) * share]
    g_wu = late[(1 + fan) * share :].reshape(fan, share, width).transpose(1, 0, 2).reshape(share, fan * width)
    return (
        mixed, input_grad,
        vec_grads[0], vec_grads[1], g_wq, vec_grads[2], g_wk, g_wv, vec_grads[3],
        late[:share], vec_grads[4], vec_grads[5], vec_grads[6],
        g_wu, g_up_bias, late[share : (1 + fan) * share], vec_grads[7],
    )


def solution(mesh):
    row, vec = P("dp", None), P("dp")
    params = (vec, vec, row, vec, row, row, vec, row, vec, vec, vec, row, vec, row, vec)
    return jax.shard_map(
        body,
        mesh=mesh,
        in_specs=(row, *params, row),
        out_specs=(row, row, *params),
        check_vma=False,
    )
```

time: 1290 us -> 632 us (0.49)
  matrix products: 425 us -> 11.1 us
  waiting for transfers between devices: 597 us -> 327 us
  Pallas kernels: 0 us -> 225 us
  other arithmetic: 121 us -> 17.2 us
  blocking collectives: 83.3 us -> 0 us
    dot_general x60 -> x3, matrix products: 425 us -> 11.1 us  [dot_tn(): lax.dot_general(left, right, (((0,), (0,)), ((), ())), preferred_element_...]
    pallas_call x0 -> x5, Pallas kernels: none -> 225 us  [the longest x1 98.9 us: feed(): pl.pallas_call(feed_kernel, grid=(count // block,), in_specs=[rows(block,...]
    reduce_scatter x6 -> x2, waiting for transfers between devices: 405 us -> 237 us  [the longest x1 144 us: body(): late = lax.psum_scatter(late, 'dp', scatter_dimension=0)]
    all_gather x6 -> x2, waiting for transfers between devices: 189 us -> 89.9 us  [the longest x1 61.3 us: body(): early = lax.all_gather(early, 'dp', axis=0)]
    unnamed x2 -> x0, blocking collectives: 83.3 us -> none
    convert_element_type x12 -> x4, other arithmetic: 65.9 us -> 2.03 us  [the longest x1 1.02 us: body(): late = late.astype(F32)]
    reduce_sum x15 -> x1, other arithmetic: 43.9 us -> 0.02 us  [body(): bias_sums = jnp.sum(bias_sums, axis=0)]
    unnamed x317 -> x25, local copies, waits for them, and re-layouts: 33.8 us -> 4.2 us
  transfers between devices with their start and end apart: 12 -> 4, of which waited for: 9 -> 4; matrix products, arithmetic and copies ran while one was open for 30% -> 3% of each run, Pallas kernels for 0% -> 8%
where the time goes in v1:
time: 632 us; the launch traced here: 631 us
  waiting for transfers between devices  327 us (52%)
  Pallas kernels  225 us (36%)
  local copies, waits for them, and re-layouts  36.4 us (6%)
  other arithmetic  17.2 us (3%)
  between operations  14 us (2%)
  matrix products  11.1 us (2%)
    reduce_scatter x1, waiting for transfers between devices, body(): late = lax.psum_scatter(late, 'dp', scatter_dimension=0)  144 us
    pallas_call x1, Pallas kernels, feed(): pl.pallas_call(feed_kernel, grid=(count // block,), in_specs=[rows(block,...  98.9 us
    reduce_scatter x1, waiting for transfers between devices, body(): early = lax.psum_scatter(early, 'dp', scatter_dimension=0).astype(F32)  93.5 us
    all_gather x1, waiting for transfers between devices, body(): early = lax.all_gather(early, 'dp', axis=0)  61.3 us
    pallas_call x1, Pallas kernels, attend_back(): pl.pallas_call(attend_back_kernel, grid=(seqs, pairs), in_specs=[block] *...  58.4 us
    pallas_call x1, Pallas kernels, attend(): pl.pallas_call(attend_kernel, grid=(seqs, pairs), in_specs=[block] * 3, o...  41.9 us
    all_gather x1, waiting for transfers between devices, body(): late = lax.all_gather(late, 'dp', axis=0)  28.6 us
    pallas_call x1, Pallas kernels, input_gradient(): pl.pallas_call(input_grad_kernel, grid=(count // block,), in_specs=[rows(...  14.3 us
  transfers between devices with their start and end apart: 4, of which 4 were waited for; matrix products, arithmetic and copies ran while one was open for 3% of the time, Pallas kernels for 8%

profile of v1, /device:TPU:0, one launch (start us, length us, event | category | flops | bytes accessed | tf_op | source)
XLA Modules:
  0.0 631.2 jit_solution(13712431647683515059)
XLA Ops:
  7.2 6.1 concatenate.23
  13.4 1.5 maximum_bitcast_fusion
  15.8 1.7 pad_maximum_fusion.2
  17.6 61.3 %all-gather.8.cloned.1.call-done = bf16[32,73,768]{2,1,0:T(8,128)(2,1)} async-done(((bf16[1,73,768]{2,1,0:T(8,128)(2,1)}), bf16[32,73,768]{2,1,0:T(8,128)(2,1)}) %all-gather.8.cloned.1.call-update) | async-done | bytes 3588112 | tf_op jit(solution)/shard_map/all_gather | solution.py:376
  81.6 2.2 fusion.5
  83.8 11.6 %project.1 = (bf16[2048,768]{1,0:T(8,128)(2,1)}, bf16[2048,768]{1,0:T(8,128)(2,1)}, bf16[2048,768]{1,0:T(8,128)(2,1)}, bf16[2048,768]{1,0:T(8,128)(2,1)}) custom-call(bf16[2048,768]{1,0:T(8,128)(2,1)} %x_ref.5, f32[8,768]{1,0:T(8,128)S(1)} %copy-done, bf16[768,768]{1,0:T(8,128)(2,1)S(1)} %bitcast.80, bf16[768,768]{1,0:T(8,128)(2,1)S(1)} %bitcast.78, ...), custom_call_target="tpu_custom_call" | custom-call | flops 7247757312 | bytes 19267584 | tf_op jit(solution)/shard_map/project/pallas_call | solution.py:61
  95.5 41.9 %attend.1 = (bf16[2048,768]{1,0:T(8,128)(2,1)S(1)}, f32[2,6,2,1024]{3,2,1,0:T(2,128)S(1)}) custom-call(bf16[2048,768]{1,0:T(8,128)(2,1)} %get-tuple-element.37.q_ref, bf16[2048,768]{1,0:T(8,128)(2,1)} %get-tuple-element.38.k_ref, bf16[2048,768]{1,0:T(8,128)(2,1)} %get-tuple-element.39.v_ref), custom_call_target="tpu_custom_call" | custom-call | flops 6442450944 | bytes 12582912 | tf_op jit(solution)/shard_map/attend/pallas_call | solution.py:121
  137.3 1.6 copy-done.3
  139.6 28.6 %all-gather.6.cloned.1.call-done = bf16[6912,768]{1,0:T(8,128)(2,1)} async-done(((bf16[216,768]{1,0:T(8,128)(2,1)}), bf16[6912,768]{1,0:T(8,128)(2,1)}) %all-gather.6.cloned.1.call-update) | async-done | bytes 10616848 | tf_op jit(solution)/shard_map/all_gather | solution.py:379
  168.2 2.4 slice.169
  170.5 6.6 %fusion.4 = (bf16[32,96,768]{2,1,0:T(8,128)(2,1)}, bf16[32,96,768]{2,1,0:T(8,128)(2,1)S(1)}) fusion(bf16[32,216,768]{2,1,0:T(8,128)(2,1)} %bitcast.85), kind=kLoop, calls=%fused_computation.33 | loop fusion | bytes 18874368 | tf_op jit(solution)/shard_map/slice | solution.py:390
  177.1 2.4 copy.60
  179.5 98.9 %feed.1 = (bf16[2048,768]{1,0:T(8,128)(2,1)}, f32[2048,768]{1,0:T(8,128)}, bf16[2048,768]{1,0:T(8,128)(2,1)}, f32[4,768]{1,0:T(4,128)}, f32[1,3072]{1,0:T(1,128)...) custom-call(bf16[2048,768]{1,0:T(8,128)(2,1)} %x_ref.5, ...), custom_call_target="tpu_custom_call" | custom-call | flops 65229815808 | bytes 43253760 | tf_op jit(solution)/shard_map/feed/pallas_call | solution.py:291
  278.5 1.3 convert.25
  282.1 58.4 %attend_back.1 = (bf16[2048,768]{1,0:T(8,128)(2,1)S(1)}, bf16[2048,768]{1,0:T(8,128)(2,1)}, bf16[2048,768]{1,0:T(8,128)(2,1)}, f32[2,2,768]{2,1,0:T(2,128)S(1)}) custom-call(bf16[2048,768]{1,0:T(8,128)(2,1)} %get-tuple-element.37.q_ref, bf16[2048,768]{1,0:T(8,128)(2,1)} %get-tuple-element.38.k_ref, bf16[2048,768]{1,0:T(8,128)(2,1)} %get-tuple-element.39.v_ref, ...), custom_call_target="tpu_custom_call" | custom-call | flops 16106127360 | bytes 22020096 | tf_op jit(solution)/shard_map/attend_back/pallas_call | solution.py:191
  340.5 3.7 convolution_convert_fusion.2
  344.2 3.7 convolution_convert_fusion
  347.9 3.7 convolution_convert_fusion.1
  351.7 14.3 %input_gradient.1 = (f32[2048,768]{1,0:T(8,128)}, f32[2,768]{1,0:T(2,128)S(1)}) custom-call(bf16[2048,768]{1,0:T(8,128)(2,1)} %x_ref.5, f32[2048,768]{1,0:T(8,128)} %get-tuple-element.42.dr_ref, bf16[2048,768]{1,0:T(8,128)(2,1)} %copy-done.2, bf16[2048,768]{1,0:T(8,128)(2,1)} %get-tuple-element.46.dk_ref, bf16[2048,768]{1,0:T(8,128)(2,1)} %get-tuple-element.47.dv_ref, ...), custom_call_target="tpu_custom_call" | custom-call | flops 7247757312 | bytes 28704768 | tf_op jit(solution)/shard_map/input_gradient/pallas_call | solution.py:342
  367.8 3.5 pad_maximum_fusion.1
  371.4 3.1 copy.63
  375.5 5.0 pad_maximum_fusion
  380.5 93.5 %reduce-scatter.3.cloned.1.call-done = bf16[1,73,768]{2,1,0:T(8,128)(2,1)} async-done(((bf16[32,73,768]{2,1,0:T(8,128)(2,1)}), bf16[1,73,768]{2,1,0:T(8,128)(2,1)}) %reduce-scatter.3.cloned.1.call-update) | async-done | bytes 112144 | tf_op jit(solution)/shard_map/reduce_scatter | solution.py:425
  476.8 143.8 %reduce-scatter.5.cloned.1.call-done = bf16[1,216,768]{2,1,0:T(8,128)(2,1)} async-done(((bf16[32,216,768]{2,1,0:T(8,128)(2,1)}), bf16[1,216,768]{2,1,0:T(8,128)(2,1)}) %reduce-scatter.5.cloned.1.call-update) | async-done | bytes 331792 | tf_op jit(solution)/shard_map/reduce_scatter | solution.py:411
  (62 shorter events, 16.6 us)
Async XLA Ops:
  7.2 71.7 %all-gather.8.cloned.1.call-start = ((), (), s32[]{:S(2)}) async-start(), calls=%async_computation.5 | async-start | bytes 4055040 | tf_op jit(solution)/shard_map/all_gather | solution.py:376
  14.8 153.3 %all-gather.6.cloned.1.call-start = ((), (), s32[]{:S(2)}) async-start(), calls=%async_computation.4 | async-start | bytes 10948608 | tf_op jit(solution)/shard_map/all_gather | solution.py:379
  17.5 456.5 %reduce-scatter.3.cloned.1.call-start = ((), (), s32[]{:S(2)}) async-start(), calls=%async_computation.2 | async-start | bytes 4055040 | tf_op jit(solution)/shard_map/reduce_scatter | solution.py:425
  81.6 2.2 copy-start
  137.3 1.6 copy-start.3
  139.0 0.6 copy-start.4
  281.2 0.9 copy-start.5
  282.1 58.4 %copy-start.7 = (bf16[2048,768]{1,0:T(8,128)(2,1)S(1)}, bf16[2048,768]{1,0:T(8,128)(2,1)}, u32[]{:S(2)}) copy-start(bf16[2048,768]{1,0:T(8,128)(2,1)} %get-tuple-element.49) | copy-start | bytes 9437188
  340.5 3.7 copy-start.2
  340.5 3.7 copy-start.9
  344.2 3.7 copy-start.8
  347.9 3.7 copy-start.1
  371.3 249.3 %reduce-scatter.5.cloned.1.call-start = ((), (), s32[]{:S(2)}) async-start(), calls=%async_computation.3 | async-start | bytes 10948608 | tf_op jit(solution)/shard_map/reduce_scatter | solution.py:411
  371.3 3.6 slice-start
  371.4 3.7 slice-start.1
  371.4 4.1 copy-start.6
Sparse Core Ops, SparseCore 0:
  15.0 63.8 all-gather.7
  82.3 85.7 all-gather.5
  371.4 102.5 reduce-scatter.2
  479.9 140.6 reduce-scatter.4
